TPU v7x, 256 devices: a whole 4x4x8 slice. The times are simulated.
256 devices in a mesh: row: 64 (over z, y, core), col: 4 (over x).
Axes of the slice: x: 4, y: 4, z: 8, core: 2. Of those that a mesh axis runs over, the one named last changes fastest.
Arguments:
- features: bfloat16 [65536, 128], P(('row', 'col')), may hold values from -6 to 6
- weight: bfloat16 [128, 256], replicated, may hold values from -0.5 to 0.5
- tiles: bfloat16 [64, 4, 384, 128, 128], P('row', 'col'), may hold values from -0.0625 to 0.0625
- tile_rows: int32 [64, 4, 384], P('row', 'col'), may hold values from 0 to 7
- tile_cols: int32 [64, 4, 384], P('row', 'col'), may hold values from 0 to 511, as said below
- tile_count: int32 [64, 4], P('row', 'col'), may hold values from 48 to 384, as said below
- block_perm: int32 [512], replicated, may hold values from 0 to 511, as said below
- cotangent: bfloat16 [65536, 256], P(('row', 'col')), may hold values from -6 to 6
Outputs:
- activation: bfloat16 [65536, 256], P(('row', 'col'))
- grad_features: float32 [65536, 128], P(('row', 'col'))
- grad_weight: float32 [128, 256], replicated
Inputs may be any that keep to these rules, and one draw needn't show every extreme that they name: `tile_cols`: on device (r, c) every slot's label lies at a block position p with (p // 2) % 4 == c, including unused slots. `tile_count`: some device is full in every draw. `block_perm`: A permutation of the node-block labels.
All inputs are finite; a program needn't handle non-finite values.
Results may differ from a plain program's by a relative error of at most 0.017.
Values may be sent and summed in bfloat16 or wider, within the bound.
A program may use at most 128 MiB of HBM per device.

v0:
```python
import jax
import jax.numpy as jnp
from jax import lax
from jax.sharding import PartitionSpec as P

slot_step = 32


def gelu_tanh(values):
    return jax.nn.gelu(values, approximate=True)


def forward_partial(tiles, rows, local, upper, gathered, rowblk, total):
    offsets = jnp.arange(slot_step, dtype=jnp.int32)
    targets = jnp.arange(rowblk, dtype=jnp.int32)

    def forward_step(index, acc):
        start = index * slot_step
        tile = lax.dynamic_slice_in_dim(tiles, start, slot_step, 0)
        where_cols = lax.dynamic_slice_in_dim(local, start, slot_step, 0)
        where_rows = lax.dynamic_slice_in_dim(rows, start, slot_step, 0)
        picked = gathered[where_cols]
        prod = jnp.einsum("tij,tjf->tif", tile, picked, preferred_element_type=jnp.float32)
        valid = start + offsets < upper
        onehot = ((where_rows[None, :] == targets[:, None]) & valid[None, :]).astype(jnp.float32)
        return acc + jnp.einsum("rt,tif->rif", onehot, prod)

    return lax.fori_loop(0, (upper + slot_step - 1) // slot_step, forward_step, total)


def backward_partial(tiles, rows, local, upper, grads, first, total):
    offsets = jnp.arange(slot_step, dtype=jnp.int32)
    blocks = total.shape[0]

    def backward_step(index, acc):
        start = index * slot_step
        tile = lax.dynamic_slice_in_dim(tiles, start, slot_step, 0)
        where_cols = lax.dynamic_slice_in_dim(local, start, slot_step, 0) - first
        where_rows = lax.dynamic_slice_in_dim(rows, start, slot_step, 0)
        picked = grads[where_rows]
        prod = jnp.einsum("tji,tjf->tif", tile, picked, preferred_element_type=jnp.float32)
        valid = (start + offsets < upper) & (where_cols >= 0) & (where_cols < blocks)
        prod = prod * valid.astype(jnp.float32)[:, None, None]
        return acc.at[jnp.clip(where_cols, 0, blocks - 1)].add(prod)

    return lax.fori_loop(0, (upper + slot_step - 1) // slot_step, backward_step, total)


def body(features, weight, tiles, tile_rows, tile_cols, tile_count, block_perm, cotangent):
    block = tiles.shape[-1]
    width = features.shape[1]
    blk_dev = features.shape[0] // block
    ncol = lax.axis_size("col")
    nrow = lax.axis_size("row")
    rowblk = blk_dev * ncol
    ncb = blk_dev * nrow
    nblk = block_perm.shape[0]
    my_tiles = tiles[0, 0]
    my_rows = tile_rows[0, 0]
    count = tile_count[0, 0]
    position = jnp.zeros((nblk,), jnp.int32).at[block_perm].set(jnp.arange(nblk, dtype=jnp.int32))
    place = position[tile_cols[0, 0]]
    local = place // (blk_dev * ncol) * blk_dev + place % blk_dev
    gathered = lax.all_gather(features, "row", axis=0, tiled=True).reshape(ncb, block, width)
    start_rows = jnp.zeros((rowblk, block, width), jnp.float32)
    partial_value = forward_partial(my_tiles, my_rows, local, count, gathered, rowblk, start_rows)
    aggregated = lax.psum_scatter(
        partial_value.reshape(rowblk * block, width), "col", scatter_dimension=0, tiled=True
    ).astype(jnp.bfloat16)
    pre = jnp.dot(aggregated, weight, preferred_element_type=jnp.float32)
    activation, pull = jax.vjp(gelu_tanh, pre)
    grad_pre = pull(cotangent.astype(jnp.float32))[0].astype(jnp.bfloat16)
    weight_term = lax.dot_general(
        aggregated, grad_pre, (((0,), (0,)), ((), ())), preferred_element_type=jnp.float32
    )
    grad_weight = lax.psum(weight_term, ("row", "col"))
    grad_agg = lax.dot_general(
        grad_pre, weight, (((1,), (1,)), ((), ())), preferred_element_type=jnp.float32
    ).astype(jnp.bfloat16)
    grads_group = lax.all_gather(grad_agg, "col", axis=0, tiled=True).reshape(rowblk, block, width)
    start_cols = jnp.zeros((ncb, block, width), jnp.float32)
    column_sum = backward_partial(my_tiles, my_rows, local, count, grads_group, 0, start_cols)
    grad_features = lax.psum_scatter(
        column_sum.reshape(ncb * block, width), "row", scatter_dimension=0, tiled=True
    )
    return (activation.astype(jnp.bfloat16), grad_features, grad_weight)


def solution(mesh):
    return jax.shard_map(
        body,
        mesh=mesh,
        in_specs=(
            P(("row", "col"), None),
            P(),
            P("row", "col", None, None, None),
            P("row", "col", None),
            P("row", "col", None),
            P("row", "col"),
            P(),
            P(("row", "col"), None),
        ),
        out_specs=(P(("row", "col"), None), P(("row", "col"), None), P()),
        check_vma=False,
    )
```

profile of v0, /device:TPU:1, one launch (start us, length us, event | category | flops | bytes accessed | tf_op | source)
XLA Modules:
  0.0 592.8 jit_solution(346610311049868025)
XLA Ops:
  10.0 2.4 scatter_custom_fusion.1
  13.2 2.8 gather_fusion.2
  16.0 78.1 %all-gather.2.cloned.1.call-done = bf16[16384,128]{1,0:T(8,128)(2,1)} async-done(((bf16[256,128]{1,0:T(8,128)(2,1)}), bf16[16384,128]{1,0:T(8,128)(2,1)}) %all-gather.2.cloned.1.call-update) | async-done | bytes 4194320 | tf_op jit(solution)/shard_map/all_gather | solution.py:64
  94.1 73.8 %while.22 = (s32[]{:T(128)}, f32[8,128,128]{2,0,1:T(8,128)S(1)}, s32[]{:T(128)}, s32[384]{0:T(512)S(1)}, s32[]{:T(128)}, /*index=5*/bf16[384,128,128]{2,1,0:T(8,...) while((s32[]{:T(128)}, f32[8,128,128]{2,0,1:T(8,128)S(1)}, ...), condition=%wide.region_2.3_spmd.clone, body=%wide.region_1.2_spmd.clone.sunk | while | flops 142739104 | bytes 7345271 | solution.py:28
  94.9 2.9 gather_fusion
  97.9 1.7 fusion.63
  101.1 2.9 gather_fusion
  104.0 1.7 fusion.63
  107.2 2.9 gather_fusion
  110.2 1.7 fusion.63
  113.4 2.9 gather_fusion
  116.3 1.7 fusion.63
  119.6 2.9 gather_fusion
  122.5 1.7 fusion.63
  125.7 2.9 gather_fusion
  128.6 1.7 fusion.63
  131.9 2.9 gather_fusion
  134.8 1.7 fusion.63
  138.0 2.9 gather_fusion
  140.9 1.7 fusion.63
  144.2 2.9 gather_fusion
  147.1 1.7 fusion.63
  150.3 2.9 gather_fusion
  153.3 1.7 fusion.63
  156.5 2.9 gather_fusion
  159.4 1.7 fusion.63
  162.6 2.9 gather_fusion
  165.6 1.7 fusion.63
  167.9 0.9 copy.15
  168.9 16.7 %copy.13 = bf16[1,1,384,128,128]{3,4,2,1,0:T(8,128)(2,1)} copy(bf16[1,1,384,128,128]{4,3,2,1,0:T(8,128)(2,1)} %bitcast.30) | data formatting | bytes 25165824 | tf_op args[2]
  185.6 2.2 reduce-scatter.3.cloned.1.call-done
  187.8 1.9 fusion.24
  189.9 1.8 fusion.32
  191.8 9.8 %all_gather.7 = bf16[1024,128]{1,0:T(8,128)(2,1)S(1)} all-gather(bf16[256,128]{1,0:T(8,128)(2,1)S(1)} %convolution_convert_fusion), channel_id=1, replica_groups=mesh['row'=64,'col'=4] {'col'}, dimensions={0}, use_global_device_ids=true | all-gather | bytes 327680 | tf_op jit(solution)/shard_map/all_gather | solution.py:80
  201.6 4.2 broadcast_in_dim.25
  205.8 113.6 %while.23 = (s32[]{:T(128)}, f32[128,128,128]{2,1,0:T(8,128)}, s32[]{:T(128)}, s32[384]{0:T(512)S(1)}, bf16[384,128,128]{1,2,0:T(8,128)(2,1)}, /*index=5*/s32[38...) while((s32[]{:T(128)}, f32[128,128,128]{2,1,0:T(8,128)}, ...), condition=%wide.region_6.7_spmd.clone, body=%wide.region_4.6_spmd.clone.sunk | while | flops 135267776 | bytes 12588471 | solution.py:46
  206.6 0.7 gather_fusion.1
  207.4 1.7 convolution_multiply_fusion.2
  209.0 6.2 %scatter_fusion = f32[128,128,128]{2,1,0:T(8,128)} fusion(f32[128,128,128]{2,1,0:T(8,128)} %get-tuple-element.350, s32[32]{0:T(128)S(1)} %get-tuple-element.299, f32[32,128,128]{2,1,0:T(8,128)S(1)} %convolution_multiply_fusion.2), kind=kCustom, calls=%fused_computation.3.clone.clone.1 | custom fusion | flops 524288 | bytes 6291584 | tf_op jit(solution)/shard_map/while/body/scatter-add | solution.py:44
  216.8 1.7 convolution_multiply_fusion.2
  218.5 6.3 %scatter_fusion = f32[128,128,128]{2,1,0:T(8,128)} fusion(f32[128,128,128]{2,1,0:T(8,128)} %get-tuple-element.350, s32[32]{0:T(128)S(1)} %get-tuple-element.299, f32[32,128,128]{2,1,0:T(8,128)S(1)} %convolution_multiply_fusion.2), kind=kCustom, calls=%fused_computation.3.clone.clone.1 | custom fusion | flops 524288 | bytes 6291584 | tf_op jit(solution)/shard_map/while/body/scatter-add | solution.py:44
  226.3 1.7 convolution_multiply_fusion.2
  228.0 6.3 %scatter_fusion = f32[128,128,128]{2,1,0:T(8,128)} fusion(f32[128,128,128]{2,1,0:T(8,128)} %get-tuple-element.350, s32[32]{0:T(128)S(1)} %get-tuple-element.299, f32[32,128,128]{2,1,0:T(8,128)S(1)} %convolution_multiply_fusion.2), kind=kCustom, calls=%fused_computation.3.clone.clone.1 | custom fusion | flops 524288 | bytes 6291584 | tf_op jit(solution)/shard_map/while/body/scatter-add | solution.py:44
  235.8 1.7 convolution_multiply_fusion.2
  237.5 6.2 %scatter_fusion = f32[128,128,128]{2,1,0:T(8,128)} fusion(f32[128,128,128]{2,1,0:T(8,128)} %get-tuple-element.350, s32[32]{0:T(128)S(1)} %get-tuple-element.299, f32[32,128,128]{2,1,0:T(8,128)S(1)} %convolution_multiply_fusion.2), kind=kCustom, calls=%fused_computation.3.clone.clone.1 | custom fusion | flops 524288 | bytes 6291584 | tf_op jit(solution)/shard_map/while/body/scatter-add | solution.py:44
  245.3 1.7 convolution_multiply_fusion.2
  246.9 6.2 %scatter_fusion = f32[128,128,128]{2,1,0:T(8,128)} fusion(f32[128,128,128]{2,1,0:T(8,128)} %get-tuple-element.350, s32[32]{0:T(128)S(1)} %get-tuple-element.299, f32[32,128,128]{2,1,0:T(8,128)S(1)} %convolution_multiply_fusion.2), kind=kCustom, calls=%fused_computation.3.clone.clone.1 | custom fusion | flops 524288 | bytes 6291584 | tf_op jit(solution)/shard_map/while/body/scatter-add | solution.py:44
  254.7 1.7 convolution_multiply_fusion.2
  256.4 6.2 %scatter_fusion = f32[128,128,128]{2,1,0:T(8,128)} fusion(f32[128,128,128]{2,1,0:T(8,128)} %get-tuple-element.350, s32[32]{0:T(128)S(1)} %get-tuple-element.299, f32[32,128,128]{2,1,0:T(8,128)S(1)} %convolution_multiply_fusion.2), kind=kCustom, calls=%fused_computation.3.clone.clone.1 | custom fusion | flops 524288 | bytes 6291584 | tf_op jit(solution)/shard_map/while/body/scatter-add | solution.py:44
  264.2 1.7 convolution_multiply_fusion.2
  265.8 6.2 %scatter_fusion = f32[128,128,128]{2,1,0:T(8,128)} fusion(f32[128,128,128]{2,1,0:T(8,128)} %get-tuple-element.350, s32[32]{0:T(128)S(1)} %get-tuple-element.299, f32[32,128,128]{2,1,0:T(8,128)S(1)} %convolution_multiply_fusion.2), kind=kCustom, calls=%fused_computation.3.clone.clone.1 | custom fusion | flops 524288 | bytes 6291584 | tf_op jit(solution)/shard_map/while/body/scatter-add | solution.py:44
  273.6 1.7 convolution_multiply_fusion.2
  275.3 6.2 %scatter_fusion = f32[128,128,128]{2,1,0:T(8,128)} fusion(f32[128,128,128]{2,1,0:T(8,128)} %get-tuple-element.350, s32[32]{0:T(128)S(1)} %get-tuple-element.299, f32[32,128,128]{2,1,0:T(8,128)S(1)} %convolution_multiply_fusion.2), kind=kCustom, calls=%fused_computation.3.clone.clone.1 | custom fusion | flops 524288 | bytes 6291584 | tf_op jit(solution)/shard_map/while/body/scatter-add | solution.py:44
  283.1 1.7 convolution_multiply_fusion.2
  284.8 6.2 %scatter_fusion = f32[128,128,128]{2,1,0:T(8,128)} fusion(f32[128,128,128]{2,1,0:T(8,128)} %get-tuple-element.350, s32[32]{0:T(128)S(1)} %get-tuple-element.299, f32[32,128,128]{2,1,0:T(8,128)S(1)} %convolution_multiply_fusion.2), kind=kCustom, calls=%fused_computation.3.clone.clone.1 | custom fusion | flops 524288 | bytes 6291584 | tf_op jit(solution)/shard_map/while/body/scatter-add | solution.py:44
  292.5 1.7 convolution_multiply_fusion.2
  294.2 6.2 %scatter_fusion = f32[128,128,128]{2,1,0:T(8,128)} fusion(f32[128,128,128]{2,1,0:T(8,128)} %get-tuple-element.350, s32[32]{0:T(128)S(1)} %get-tuple-element.299, f32[32,128,128]{2,1,0:T(8,128)S(1)} %convolution_multiply_fusion.2), kind=kCustom, calls=%fused_computation.3.clone.clone.1 | custom fusion | flops 524288 | bytes 6291584 | tf_op jit(solution)/shard_map/while/body/scatter-add | solution.py:44
  302.0 1.7 convolution_multiply_fusion.2
  303.7 6.3 %scatter_fusion = f32[128,128,128]{2,1,0:T(8,128)} fusion(f32[128,128,128]{2,1,0:T(8,128)} %get-tuple-element.350, s32[32]{0:T(128)S(1)} %get-tuple-element.299, f32[32,128,128]{2,1,0:T(8,128)S(1)} %convolution_multiply_fusion.2), kind=kCustom, calls=%fused_computation.3.clone.clone.1 | custom fusion | flops 524288 | bytes 6291584 | tf_op jit(solution)/shard_map/while/body/scatter-add | solution.py:44
  311.5 1.7 convolution_multiply_fusion.2
  313.1 6.3 %scatter_fusion = f32[128,128,128]{2,1,0:T(8,128)} fusion(f32[128,128,128]{2,1,0:T(8,128)} %get-tuple-element.350, s32[32]{0:T(128)S(1)} %get-tuple-element.299, f32[32,128,128]{2,1,0:T(8,128)S(1)} %convolution_multiply_fusion.2), kind=kCustom, calls=%fused_computation.3.clone.clone.1 | custom fusion | flops 524288 | bytes 6291584 | tf_op jit(solution)/shard_map/while/body/scatter-add | solution.py:44
  319.4 116.7 %all-reduce.2.cloned.1.call-done = f32[128,256]{1,0:T(8,128)} async-done(((f32[128,256]{1,0:T(8,128)}), f32[128,256]{1,0:T(8,128)}) %all-reduce.2.cloned.1.call-update) | async-done | bytes 131088 | tf_op jit(solution)/shard_map/psum | solution.py:76
  436.2 148.5 %reduce-scatter.5.cloned.1.call-done = f32[256,128]{1,0:T(8,128)} async-done(((f32[16384,128]{1,0:T(8,128)}), f32[256,128]{1,0:T(8,128)}) %reduce-scatter.5.cloned.1.call-update) | async-done | bytes 131088 | tf_op jit(solution)/shard_map/reduce_scatter | solution.py:83
  584.7 1.6 copy.39
  (127 shorter events, 39.2 us)
Async XLA Ops:
  7.2 180.7 %copy-start = (bf16[128,256]{1,0:T(8,128)(2,1)S(1)}, bf16[128,256]{1,0:T(8,128)(2,1)}, u32[]{:S(2)}) copy-start(bf16[128,256]{1,0:T(8,128)(2,1)} %param.13) | copy-start | bytes 196612
  7.2 86.9 %all-gather.2.cloned.1.call-start = ((), (), s32[]{:S(2)}) async-start(), calls=%async_computation.2 | async-start | bytes 4259840 | tf_op jit(solution)/shard_map/all_gather | solution.py:64
  7.9 179.9 %reduce-scatter.3.cloned.1.call-start = ((), (), s32[]{:S(2)}) async-start(), calls=%async_computation.3 | async-start | bytes 655360 | tf_op jit(solution)/shard_map/reduce_scatter | solution.py:67
  168.9 267.3 %all-reduce.2.cloned.1.call-start = ((), (), s32[]{:S(2)}) async-start(), calls=%async_computation.5 | async-start | bytes 262144 | tf_op jit(solution)/shard_map/psum | solution.py:76
  168.9 18.9 %copy-start.1 = (bf16[256,256]{1,0:T(8,128)(2,1)S(1)}, bf16[256,256]{1,0:T(8,128)(2,1)}, u32[]{:S(2)}) copy-start(bf16[256,256]{1,0:T(8,128)(2,1)} %param.19) | copy-start | bytes 393220
  191.7 393.0 %reduce-scatter.5.cloned.1.call-start = ((), (), s32[]{:S(2)}) async-start(), calls=%async_computation.4 | async-start | bytes 8519680 | tf_op jit(solution)/shard_map/reduce_scatter | solution.py:83
Sparse Core Ops, SparseCore 0:
  10.8 83.2 all-gather.1
  169.0 18.7 reduce-scatter.2
  193.9 242.2 all-reduce.1
  440.8 143.8 reduce-scatter.4
where the time goes:
time: 601 us; the launch traced here: 593 us
  waiting for transfers between devices  346 us (58%)
  other arithmetic  95.5 us (16%)
  local copies, waits for them, and re-layouts  73.8 us (12%)
  matrix products  52 us (9%)
  between operations  14.5 us (2%)
  blocking collectives  9.79 us (2%)
    reduce_scatter x1, waiting for transfers between devices, body(): lax.psum_scatter(column_sum.reshape(ncb * block, width), 'row', scatter_d...  149 us
    psum x1, waiting for transfers between devices, body(): grad_weight = lax.psum(weight_term, ('row', 'col'))  117 us
    all_gather x1, waiting for transfers between devices, body(): lax.all_gather(features, 'row', axis=0, tiled=True)  78.1 us
    scatter-add x12, other arithmetic, backward_step(): return acc.at[jnp.clip(where_cols, 0, blocks - 1)].add(prod)  74.8 us
    gather x12, local copies, waits for them, and re-layouts, forward_step(): picked = gathered[where_cols]  35.2 us
    dot_general x12, matrix products, backward_step(): jnp.einsum('tji,tjf->tif', tile, picked, preferred_element_type=jnp.float32)  19.9 us
    dot_general x12, matrix products, forward_step(): jnp.einsum('tij,tjf->tif', tile, picked, preferred_element_type=jnp.float32)  19.9 us
    unnamed x6, local copies, waits for them, and re-layouts  18.3 us
  transfers between devices with their start and end apart: 4, of which 4 were waited for; matrix products, arithmetic and copies ran while one was open for 24% of the time, Pallas kernels for 0%

commit v1 on v0

v1 whole, which is shorter than its diff:
```python
import math

import jax
import jax.numpy as jnp
from jax import lax
from jax.experimental import pallas as pl
from jax.experimental.pallas import tpu as pltpu
from jax.sharding import PartitionSpec as P

MESH = pl.DeviceIdType.MESH
BF = jnp.bfloat16
F32 = jnp.float32

NZ, NY, NX = 8, 4, 4
BS, F, H = 128, 128, 256
TCAP, NBLK, ROWBLK = 384, 512, 8
NPLACE = 1024
ROWS = 256
G1, G2A, G2 = 176, 48, 80
R1, R2A, R2 = 96, 16, 32
NSEM = 256
GELU = math.sqrt(2.0 / math.pi)


class Sends:
    def __init__(self, send_sem, recv_sem, device):
        self.send_sem, self.recv_sem, self.device = send_sem, recv_sem, device
        self.count, self.started, self.landing = 0, [], {}

    def describe(self, number, source, target, device):
        return pltpu.make_async_remote_copy(
            src_ref=source, dst_ref=target, send_sem=self.send_sem.at[number],
            recv_sem=self.recv_sem.at[number], device_id=device, device_id_type=MESH)

    def start(self, name, source, target, device):
        copy = self.describe(self.count, source, target, device)
        copy.start()
        self.started.append(copy)
        self.landing[name] = (self.count, target)
        self.count += 1

    def wait(self, name):
        number, target = self.landing.pop(name)
        self.describe(number, target, target, self.device).wait_recv()

    def drain(self):
        for copy in self.started:
            copy.wait_send()


def prepare(rows_ref, cols_ref, count_ref, perm_ref, table):
    def iota(shape, dim):
        return lax.broadcasted_iota(jnp.int32, shape, dim)

    def total(picked, values, axis):
        return jnp.sum(jnp.where(picked, values, 0), axis=axis, keepdims=True)

    square = (TCAP, TCAP)
    sub, lane = iota(square, 0), iota(square, 1)
    cols = total(sub == lane, cols_ref[...], 1)
    rows = total(sub == lane, rows_ref[...], 1)
    spot = total(perm_ref[...] == cols, iota((TCAP, NBLK), 1), 1)
    key = rows * 128 + spot // 8 * 2 + spot % 2
    key = jnp.where(iota((TCAP, 1), 0) < count_ref[0, 0], key, 2048)
    flat = total(sub == lane, key, 0)
    ahead = (flat < key) | ((flat == key) & (lane < sub))
    rank = total(ahead, 1, 1)
    order = total(rank == lane, sub, 0)
    keys = total(rank == lane, key, 0)
    place = iota((TCAP, NPLACE), 1)
    upto = total(key <= place, 1, 0)
    here = total(key == place, 1, 0)
    last = jnp.where(here > 0, upto - 1, TCAP)
    table[...] = jnp.zeros_like(table)
    table[0:1, :] = jnp.clip(last, 0, TCAP)
    table[1:2, 0:TCAP] = jnp.clip(order, 0, TCAP - 1)
    table[2:3, 0:TCAP] = keys


def pick(index, line, number, most):
    return jnp.minimum(jnp.maximum(index[line, number], 0), most)


def merge(index, raw, merged):
    def step(number, carry):
        total, before = carry
        mine = index[2, number]
        keep = jnp.where(mine == before, 1.0, 0.0).astype(F32)
        total = raw[pick(index, 1, number, TCAP - 1)].astype(F32) + total * keep
        merged[number] = total.astype(BF)
        return total, mine

    lax.fori_loop(0, TCAP, step, (jnp.zeros((BS, BS), F32), jnp.int32(-1)))
    merged[TCAP] = jnp.zeros((BS, BS), BF)


def whole(
    features, weight, tiles, rows_ref, cols_ref, count_ref, perm_ref, cotangent,
    activation, grad_features, grad_weight,
    raw, merged, table, index, near, acc, part, part_in, gt, twin, twin_in, summed,
    y_in, z_out, z_in, far_in, half_in, relay, relay_in, q_out, q_in,
    w1, w1_in, w2, w2_in, w3, w4, w5, local_sem, send_sem, recv_sem,
):
    row, x = lax.axis_index("row"), lax.axis_index("col")
    z, y, core = row // (2 * NY), (row // 2) % NY, row % 2

    def device(dz, dy, dc=0, dx=0):
        there = ((z + dz + NZ) % NZ * NY + (y + dy + NY) % NY) * 2 + (core + dc) % 2
        return there, (x + dx) % NX

    mine8 = y * 2 + core

    def octet(step):
        there = (mine8 + step) % 8
        return (z * NY + there // 2) * 2 + there % 2, x

    fetches = []
    for part_no in range(8):
        some = pl.ds(part_no * (TCAP // 8), TCAP // 8)
        fetches.append(pltpu.make_async_copy(tiles.at[0, 0, some], raw.at[some], local_sem.at[part_no]))
        fetches[-1].start()
    barrier = pltpu.get_barrier_semaphore()
    peers = [device(dz, 0) for dz in range(1, NZ)] + [octet(step) for step in range(1, 8)]
    peers += [device(0, 0, 0, dx) for dx in range(1, NX)]
    for peer in peers:
        pl.semaphore_signal(barrier, inc=1, device_id=peer, device_id_type=MESH)

    prepare(rows_ref, cols_ref, count_ref, perm_ref, table)
    to_scalar = pltpu.make_async_copy(table, index, local_sem.at[8])
    to_scalar.start()
    acc[...] = jnp.zeros_like(acc)
    near[0, 0, 0] = features[...]
    to_scalar.wait()
    for fetch in fetches:
        fetch.wait()
    merge(index, raw, merged)
    pl.semaphore_wait(barrier, len(peers))

    sends = Sends(send_sem, recv_sem, device(0, 0, 1))
    sibling = device(0, 0, 1)

    def block(oz, oy, piece):
        return near.at[oz % NZ, oy % NY, 0, pl.ds(piece[0], piece[1]), :]

    g1, g2, g2a, g2b = (0, G1), (G1, G2), (G1, G2A), (G1 + G2A, G2 - G2A)

    def pass_on(name, oz, oy, piece, dz, dy):
        source = features.at[pl.ds(piece[0], piece[1]), :] if (oz, oy) == (0, 0) else block(oz, oy, piece)
        sends.start(name, source, block(oz - dz, oy - dy, piece), device(dz, dy))

    def along_y(oz):
        for dy in (1, -1, 2):
            pass_on(("y", oz, dy), oz, 0, g1, 0, dy)

    def along_y_done(oz):
        for dy in (1, -1, 2):
            sends.wait(("y", oz, dy))

    def along_z(oy):
        for dz in (1, -1, 2, -2):
            pass_on(("q", oy, dz), 0, oy, g2, dz, 0)

    def along_z_more(oy):
        for s, half in ((1, g2a), (-1, g2b)):
            sends.wait(("q", oy, s))
            sends.wait(("q", oy, 2 * s))
            pass_on(("q", oy, 3 * s), -2 * s, oy, g2, s, 0)
            pass_on(("q", oy, 4 * s), -2 * s, oy, half, 2 * s, 0)

    def share(oz):
        sends.start(("s", oz), near.at[oz % NZ, :, 0], near.at[oz % NZ, :, 1], sibling)

    def column(dzi, dyi, other):
        there = (((z + dzi) % NZ) * NY + (y + dyi) % NY) * 2 + (core + other) % 2
        return there * 2

    def forward(first, second, other):
        def step(number, carry):
            dzi = first + (second - first) * (number // NY)
            dyi = number % NY
            where = column(dzi, dyi, other)
            block_in = near[dzi, dyi, other]
            for rb in range(ROWBLK):
                left = merged[pick(index, 0, rb * 128 + where, TCAP)]
                right = merged[pick(index, 0, rb * 128 + where + 1, TCAP)]
                acc[rb] += jnp.dot(jnp.concatenate([left, right], axis=1), block_in, preferred_element_type=F32)
            return carry

        lax.fori_loop(0, NY if first == second else 2 * NY, step, 0)

    for s in (1, -1):
        pass_on(("z", s), 0, 0, g1, s, 0)
        pass_on(("p", s), 0, 0, g2, 0, s)
    for s in (1, -1):
        pass_on(("z", 2 * s), 0, 0, g1, 2 * s, 0)
    pass_on(("p", 2), 0, 0, g2, 0, 2)
    along_y(0)
    for s in (1, -1):
        pass_on(("z", 3 * s), 0, 0, g1, 3 * s, 0)
    pass_on(("z", 4), 0, 0, g1, 4, 0)
    along_z(0)
    for s in (1, -1):
        sends.wait(("z", s))
        along_y(-s)
    for s in (1, -1):
        sends.wait(("p", s))
        along_z(-s)
    for s in (1, -1):
        sends.wait(("z", 2 * s))
        along_y(-2 * s)
    sends.wait(("p", 2))
    along_z(-2)
    for s in (1, -1):
        sends.wait(("z", 3 * s))
        along_y(-3 * s)
    sends.wait(("z", 4))
    along_y(-4)
    along_y_done(0)
    share(0)
    along_z_more(0)
    forward(0, 0, 0)
    along_z_more(-1)
    along_z_more(1)
    along_z_more(-2)
    for oz in (-1, 1):
        along_y_done(oz)
        share(oz)
    sends.wait(("s", 0))
    forward(0, 0, 1)
    forward(1, 7, 0)
    for oz in (-2, 2):
        along_y_done(oz)
        share(oz)
    sends.wait(("s", 1))
    sends.wait(("s", -1))
    forward(1, 7, 1)
    forward(2, 6, 0)
    for oy in (0, -1, 1, -2):
        sends.wait(("q", oy, 3))
        sends.wait(("q", oy, -3))
    for oz in (-3, 3):
        along_y_done(oz)
        share(oz)
    sends.wait(("s", 2))
    sends.wait(("s", -2))
    forward(2, 6, 1)
    forward(3, 5, 0)
    for oy in (0, -1, 1, -2):
        sends.wait(("q", oy, 4))
        sends.wait(("q", oy, -4))
    along_y_done(-4)
    share(4)
    sends.wait(("s", 3))
    sends.wait(("s", -3))
    forward(3, 5, 1)
    forward(4, 4, 0)
    sends.wait(("s", 4))
    forward(4, 4, 1)

    for dx in (2, 1, 3):
        there = (x + dx) % NX
        part[dx] = acc[pl.ds(there * 2, 2)].reshape(ROWS, F).astype(BF)
        sends.start(("part", dx), part.at[dx], part_in.at[dx], device(0, 0, 0, dx))
    total = acc[pl.ds(x * 2, 2)].reshape(ROWS, F)
    for dx in (1, 3, 2):
        sends.wait(("part", dx))
        total += part_in[dx].astype(F32)
    aggregated = total.astype(BF)
    pre = jnp.dot(aggregated, weight[...], preferred_element_type=F32)
    square = pre * pre
    bend = jnp.tanh(GELU * (pre + 0.044715 * (square * pre)))
    slope = 0.5 * (1.0 + bend) + (0.5 * GELU) * pre * (1.0 - bend * bend) * (1.0 + 3.0 * 0.044715 * square)
    grad_pre = (cotangent[...].astype(F32) * slope).astype(BF)
    gt[0] = lax.dot_general(weight[...], grad_pre, (((1,), (1,)), ((), ())), preferred_element_type=F32).astype(BF)
    for dx in (2, 1, 3):
        sends.start(("gt", dx), gt.at[0], gt.at[NX - dx], device(0, 0, 0, dx))
    activation[...] = (0.5 * pre * (1.0 + bend)).astype(BF)
    term = lax.dot_general(aggregated, grad_pre, (((0,), (0,)), ((), ())), preferred_element_type=F32)
    for q in range(NX):
        for j in range(8):
            w1[q, j] = term[q * 32 + j % 4 * 8:q * 32 + j % 4 * 8 + 8, j // 4 * 128:j // 4 * 128 + 128]
    for dx in (2, 1, 3):
        sends.start(("w1", dx), w1.at[(x + dx) % NX], w1_in.at[dx], device(0, 0, 0, dx))
    for dx in (1, 3, 2):
        sends.wait(("gt", dx))

    def backward(first, second, other):
        def step(number, carry):
            dzi = first + (second - first) * (number // NY)
            dyi = number % NY
            where = column(dzi, dyi, other)
            sum_ = jnp.zeros((F, ROWS), F32)
            for dx in range(NX):
                base = (x + dx) % NX * 2 * 128 + where
                corners = [merged[pick(index, 0, base + a, TCAP)] for a in (0, 1, 128, 129)]
                grid = jnp.concatenate([jnp.concatenate(corners[:2], axis=1), jnp.concatenate(corners[2:], axis=1)], axis=0)
                sum_ += jnp.dot(gt[dx], grid, preferred_element_type=F32)
            if other:
                twin[dzi, dyi] = sum_.astype(BF)
            else:
                summed[dzi, dyi] = (sum_ + twin_in[dzi, dyi].astype(F32)).astype(BF)
            return carry

        lax.fori_loop(0, NY if first == second else 2 * NY, step, 0)

    r1, r2, r2a, r2b = pl.ds(0, R1), pl.ds(R1, R2), pl.ds(R1, R2A), pl.ds(R1 + R2A, R2 - R2A)
    dys = (1, 3, 2)

    def for_twin(*group):
        backward(group[0], group[-1], 1)
        for dzi in group:
            sends.start(("t", dzi), twin.at[dzi], twin_in.at[dzi], sibling)

    def for_plane(*group):
        for dzi in group:
            sends.wait(("t", dzi))
        backward(group[0], group[-1], 0)
        for dzi in group:
            for k, dy in enumerate(dys):
                sends.start(("Y", dzi, k), summed.at[dzi, dy, r1], y_in.at[dzi, k], device(0, dy))
        for dzi in group:
            for dy in range(NY):
                if dzi == 4:
                    sends.start(("half", 0, dy), summed.at[4, dy, r2a], half_in.at[0, dy, pl.ds(0, R2A)], device(2, 0))
                    sends.start(("half", 1, dy), summed.at[4, dy, r2b], half_in.at[1, dy, pl.ds(0, R2 - R2A)], device(-2, 0))
                elif dzi in (3, 5):
                    s = 0 if dzi == 3 else 1
                    sends.start(("far", s, dy), summed.at[dzi, dy, r2], far_in.at[s, dy], device(1 - 2 * s, 0))
                elif dzi in (1, 7):
                    s = 0 if dzi == 1 else 1
                    sends.start(("q", s, dy), summed.at[dzi, dy, r2], relay_in.at[s, dy], device(1 - 2 * s, 0))

    def relays():
        for s, dzi in ((0, 2), (1, 6)):
            for dy in (1, 3, 2, 0):
                sends.wait(("half", s, dy))
                sends.wait(("far", s, dy))
                relay[s, dy] = (summed[dzi, dy, r2].astype(F32) + far_in[s, dy].astype(F32)).astype(BF)
                some = pl.ds(0, R2A) if s == 0 else pl.ds(R2A, R2 - R2A)
                extra = half_in[s, dy, pl.ds(0, R2A if s == 0 else R2 - R2A)]
                mine = r2a if s == 0 else r2b
                relay[s, dy, some] = (
                    summed[dzi, dy, mine].astype(F32) + far_in[s, dy, some].astype(F32) + extra.astype(F32)
                ).astype(BF)
                sends.start(("q", 2 + s, dy), relay.at[s, dy], relay_in.at[2 + s, dy], device(2 - 4 * s, 0))

    def y_sum(dzi):
        value = summed[dzi, 0, r1].astype(F32)
        for k in range(3):
            sends.wait(("Y", dzi, k))
            value += y_in[dzi, k].astype(F32)
        return value

    def z_stage(dzi):
        z_out[dzi] = y_sum(dzi).astype(BF)
        sends.start(("Z", dzi), z_out.at[dzi], z_in.at[dzi], device(dzi, 0))

    def q_sum(dy):
        value = summed[0, dy, r2].astype(F32)
        for k in range(4):
            sends.wait(("q", k, dy))
            value += relay_in[k, dy].astype(F32)
        return value

    for_twin(4)
    for_twin(3, 5)
    for_plane(4)
    for_twin(2, 6)
    for_plane(3, 5)
    w2[...] = w1[x]
    for dx in (1, 3, 2):
        sends.wait(("w1", dx))
        w2[...] += w1_in[dx]
    for step in range(1, 8):
        sends.start(("w2", step), w2.at[(mine8 + step) % 8], w2_in.at[step], octet(step))
    for_twin(1, 7)
    for_plane(2, 6)
    z_stage(4)
    relays()
    for_twin(0)
    for_plane(1, 7)
    z_stage(3)
    z_stage(5)
    here = w2[mine8]
    for step in range(1, 8):
        sends.wait(("w2", step))
        here += w2_in[step]
    w3[z] = here
    for dz in range(1, NZ):
        sends.start(("w3", dz), w3.at[z], w3.at[z], device(dz, 0))
    for_plane(0)
    for dzi in (2, 6, 1, 7):
        z_stage(dzi)
    for k, dy in enumerate(dys):
        q_out[k] = q_sum(dy).astype(BF)
        sends.start(("Q", k), q_out.at[k], q_in.at[k], device(0, dy))
    for dz in range(1, NZ):
        number, _ = sends.landing.pop(("w3", dz))
        source = w3.at[(z + NZ - dz) % NZ]
        sends.describe(number, source, source, sibling).wait_recv()
    here = w3[0]
    for k in range(1, NZ):
        here += w3[k]
    w4[mine8] = here
    for step in range(1, 8):
        sends.start(("w4", step), w4.at[mine8], w4.at[mine8], octet(step))
    top = y_sum(0)
    bottom = q_sum(0)
    for step in range(1, 8):
        number, _ = sends.landing.pop(("w4", step))
        source = w4.at[(mine8 + 8 - step) % 8]
        sends.describe(number, source, source, sibling).wait_recv()
    w5[x] = w4[...]
    for dx in (2, 1, 3):
        sends.start(("w5", dx), w4, w5.at[x], device(0, 0, 0, dx))
    for dzi in (4, 3, 5, 2, 6, 1, 7):
        sends.wait(("Z", dzi))
        top += z_in[dzi].astype(F32)
    for k in range(3):
        sends.wait(("Q", k))
        bottom += q_in[k].astype(F32)
    grad_features[...] = jnp.concatenate([top, bottom], axis=0).T
    for dx in (1, 3, 2):
        number, _ = sends.landing.pop(("w5", dx))
        source = w5.at[(x + NX - dx) % NX]
        sends.describe(number, source, source, sibling).wait_recv()
    for q in range(NX):
        for j in range(8):
            grad_weight[pl.ds(q * 32 + j % 4 * 8, 8), pl.ds(j // 4 * 128, 128)] = w5[q, j]
    sends.drain()
    assert not sends.landing


def body(features, weight, tiles, tile_rows, tile_cols, tile_count, block_perm, cotangent):
    vmem = pl.BlockSpec(memory_space=pltpu.VMEM)
    smem = pl.BlockSpec(memory_space=pltpu.SMEM)
    return pl.pallas_call(
        whole,
        out_shape=(
            jax.ShapeDtypeStruct((ROWS, H), BF),
            jax.ShapeDtypeStruct((ROWS, F), F32),
            jax.ShapeDtypeStruct((F, H), F32),
        ),
        in_specs=[vmem, vmem, pl.BlockSpec(memory_space=pl.ANY), vmem, vmem, smem, vmem, vmem],
        out_specs=(vmem, vmem, vmem),
        scratch_shapes=[
            pltpu.VMEM((TCAP, BS, BS), BF),
            pltpu.VMEM((TCAP + 1, BS, BS), BF),
            pltpu.VMEM((8, NPLACE), jnp.int32),
            pltpu.SMEM((8, NPLACE), jnp.int32),
            pltpu.VMEM((NZ, NY, 2, ROWS, F), BF),
            pltpu.VMEM((ROWBLK, BS, F), F32),
            pltpu.VMEM((NX, ROWS, F), BF),
            pltpu.VMEM((NX, ROWS, F), BF),
            pltpu.VMEM((NX, F, ROWS), BF),
            pltpu.VMEM((NZ, NY, F, ROWS), BF),
            pltpu.VMEM((NZ, NY, F, ROWS), BF),
            pltpu.VMEM((NZ, NY, F, ROWS), BF),
            pltpu.VMEM((NZ, 3, R1, ROWS), BF),
            pltpu.VMEM((NZ, R1, ROWS), BF),
            pltpu.VMEM((NZ, R1, ROWS), BF),
            pltpu.VMEM((2, NY, R2, ROWS), BF),
            pltpu.VMEM((2, NY, R2A, ROWS), BF),
            pltpu.VMEM((2, NY, R2, ROWS), BF),
            pltpu.VMEM((4, NY, R2, ROWS), BF),
            pltpu.VMEM((3, R2, ROWS), BF),
            pltpu.VMEM((3, R2, ROWS), BF),
            pltpu.VMEM((NX, 8, 8, 128), F32),
            pltpu.VMEM((NX, 8, 8, 128), F32),
            pltpu.VMEM((8, 8, 128), F32),
            pltpu.VMEM((8, 8, 128), F32),
            pltpu.VMEM((NZ, 8, 128), F32),
            pltpu.VMEM((8, 8, 128), F32),
            pltpu.VMEM((NX, 8, 8, 128), F32),
            pltpu.SemaphoreType.DMA((9,)),
            pltpu.SemaphoreType.DMA((NSEM,)),
            pltpu.SemaphoreType.DMA((NSEM,)),
        ],
        compiler_params=pltpu.CompilerParams(
            collective_id=0, has_side_effects=True, vmem_limit_bytes=56 * 2**20),
    )(
        features, weight, tiles, tile_rows.reshape(1, TCAP), tile_cols.reshape(1, TCAP), tile_count,
        block_perm.reshape(1, NBLK), cotangent,
    )


def solution(mesh):
    return jax.shard_map(
        body,
        mesh=mesh,
        in_specs=(
            P(("row", "col"), None),
            P(),
            P("row", "col", None, None, None),
            P("row", "col", None),
            P("row", "col", None),
            P("row", "col"),
            P(),
            P(("row", "col"), None),
        ),
        out_specs=(P(("row", "col"), None), P(("row", "col"), None), P()),
        check_vma=False,
    )
```

time: 601 us -> 109 us (0.18); the launches traced: 593 us -> 109 us
  waiting for transfers between devices: 346 us -> 0 us
  Pallas kernels: 0 us -> 103 us
  other arithmetic: 95.5 us -> 0 us
  local copies, waits for them, and re-layouts: 73.8 us -> 4.7 us
  matrix products: 52 us -> 0 us
  between operations: 14.5 us -> 1.29 us
  blocking collectives: 9.79 us -> 0 us
    reduce_scatter x2 -> x0, waiting for transfers between devices: 151 us -> none  [the longest x1 149 us: body(): lax.psum_scatter(column_sum.reshape(ncb * block, width), 'row', scatter_d...]
    psum x1 -> x0, waiting for transfers between devices: 117 us -> none  [body(): grad_weight = lax.psum(weight_term, ('row', 'col'))]
    pallas_call x0 -> x1, Pallas kernels: none -> 103 us  [body(): pl.pallas_call(whole, out_shape=(jax.ShapeDtypeStruct((ROWS, H), BF), jax...]
    all_gather x1 -> x0, waiting for transfers between devices: 78.1 us -> none  [body(): lax.all_gather(features, 'row', axis=0, tiled=True)]
    scatter-add x12 -> x0, other arithmetic: 74.8 us -> none  [backward_step(): return acc.at[jnp.clip(where_cols, 0, blocks - 1)].add(prod)]
    dot_general x39 -> x0, matrix products: 52 us -> none  [the longest x12 19.9 us: backward_step(): jnp.einsum('tji,tjf->tif', tile, picked, preferred_element_type=jnp.float32)]
    gather x25 -> x0, local copies, waits for them, and re-layouts: 47 us -> none  [the longest x12 35.2 us: forward_step(): picked = gathered[where_cols]]
    unnamed x6 -> x3, local copies, waits for them, and re-layouts: 18.3 us -> 4.7 us
  transfers between devices with their start and end apart: 4 -> 0, of which waited for: 4 -> 0; matrix products, arithmetic and copies ran while one was open for 24% -> 0% of each run, Pallas kernels for 0% -> 0%
where the time goes in v1:
time: 109 us
  Pallas kernels  103 us (94%)
  local copies, waits for them, and re-layouts  4.7 us (4%)
  between operations  1.29 us (1%)
    pallas_call x1, Pallas kernels, body(): pl.pallas_call(whole, out_shape=(jax.ShapeDtypeStruct((ROWS, H), BF), jax...  103 us
    unnamed x3, local copies, waits for them, and re-layouts  4.7 us

profile of v1, /device:TPU:1, one launch (start us, length us, event | category | flops | bytes accessed | tf_op | source)
XLA Modules:
  0.0 109.3 jit_solution(12122135075626330100)
XLA Ops:
  1.3 103.3 %shard_map.103 = (bf16[256,256]{1,0:T(8,128)(2,1)}, f32[256,128]{1,0:T(8,128)}, f32[128,256]{1,0:T(8,128)}) custom-call(bf16[256,128]{1,0:T(8,128)(2,1)} %features.1, bf16[128,256]{1,0:T(8,128)(2,1)} %weight.1, bf16[1,1,384,128,128]{4,3,2,1,0:T(8,128)(2,1)} %tiles.1, s32[1,384]{1,0:T(1,128)} %bitcast.4, s32[1,384]{1,0:T(1,128)} %bitcast.5, ...), custom_call_target="tpu_custom_call" | custom-call | tf_op jit(solution)/shard_map/pallas_call | solution.py:437
  104.6 1.6 %copy.15 = bf16[256,256]{1,0:T(8,128)(2,1)} copy(bf16[256,256]{1,0:T(8,128)(2,1)} %get-tuple-element.6) | data formatting | bytes 262144
  106.1 1.6 %copy.16 = f32[256,128]{1,0:T(8,128)} copy(f32[256,128]{1,0:T(8,128)} %get-tuple-element.7) | data formatting | bytes 262144
  107.7 1.6 %copy.17 = f32[128,256]{1,0:T(8,128)} copy(f32[128,256]{1,0:T(8,128)} %get-tuple-element.8) | data formatting | bytes 262144

commit v2 on v1

v2 whole, which is shorter than its diff:
```python
import math

import jax
import jax.numpy as jnp
from jax import lax
from jax.experimental import pallas as pl
from jax.experimental.pallas import tpu as pltpu
from jax.sharding import PartitionSpec as P

MESH = pl.DeviceIdType.MESH
BF = jnp.bfloat16
F32 = jnp.float32

NZ, NY, NX = 8, 4, 4
BS, F, H = 128, 128, 256
TCAP, NBLK, ROWBLK = 384, 512, 8
NPLACE = 1024
ROWS = 256
G1, G1A, G2A, G2 = 176, 80, 48, 80
R1, R1A, R2A, R2 = 80, 32, 16, 48
NSEM = 256
GELU = math.sqrt(2.0 / math.pi)


class Sends:
    def __init__(self, send_sem, recv_sem, device):
        self.send_sem, self.recv_sem, self.device = send_sem, recv_sem, device
        self.count, self.started, self.landing = 0, [], {}

    def describe(self, number, source, target, device):
        return pltpu.make_async_remote_copy(
            src_ref=source, dst_ref=target, send_sem=self.send_sem.at[number],
            recv_sem=self.recv_sem.at[number], device_id=device, device_id_type=MESH)

    def start(self, name, source, target, device):
        copy = self.describe(self.count, source, target, device)
        copy.start()
        self.started.append(copy)
        self.landing[name] = (self.count, target)
        self.count += 1

    def wait(self, name):
        self.wait_for(name, self.landing[name][1])

    def wait_for(self, name, target):
        number, _ = self.landing.pop(name)
        self.describe(number, target, target, self.device).wait_recv()

    def drain(self):
        for copy in self.started:
            copy.wait_send()


def prepare(rows_ref, cols_ref, count_ref, perm_ref, table):
    def iota(shape, dim):
        return lax.broadcasted_iota(jnp.int32, shape, dim)

    def total(picked, values, axis):
        return jnp.sum(jnp.where(picked, values, 0), axis=axis, keepdims=True)

    square = (TCAP, TCAP)
    sub, lane = iota(square, 0), iota(square, 1)
    cols = total(sub == lane, cols_ref[...], 1)
    rows = total(sub == lane, rows_ref[...], 1)
    spot = total(perm_ref[...] == cols, iota((TCAP, NBLK), 1), 1)
    key = rows * 128 + spot // 8 * 2 + spot % 2
    key = jnp.where(iota((TCAP, 1), 0) < count_ref[...], key, 2048)
    flat = total(sub == lane, key, 0)
    ahead = (flat < key) | ((flat == key) & (lane < sub))
    rank = total(ahead, 1, 1)
    order = total(rank == lane, sub, 0)
    keys = total(rank == lane, key, 0)
    place = iota((TCAP, NPLACE), 1)
    upto = total(key <= place, 1, 0)
    here = total(key == place, 1, 0)
    last = jnp.where(here > 0, upto - 1, TCAP)
    table[...] = jnp.zeros_like(table)
    table[0:1, :] = jnp.clip(last, 0, TCAP)
    table[1:2, 0:TCAP] = jnp.clip(order, 0, TCAP - 1)
    table[2:3, 0:TCAP] = keys


def pick(index, line, number, most):
    return jnp.minimum(jnp.maximum(index[line, number], 0), most)


def merge(index, raw, merged):
    def step(number, carry):
        total, before = carry
        mine = index[2, number]
        keep = jnp.where(mine == before, 1.0, 0.0).astype(F32)
        total = raw[pick(index, 1, number, TCAP - 1)].astype(F32) + total * keep
        merged[number] = total.astype(BF)
        return total, mine

    lax.fori_loop(0, TCAP, step, (jnp.zeros((BS, BS), F32), jnp.int32(-1)), unroll=8)
    merged[TCAP] = jnp.zeros((BS, BS), BF)


def whole(
    features, weight_in, tiles, rows_in, cols_in, count_in, perm_in, cotangent_in,
    activation, grad_turned, w5,
    weight, rows_ref, cols_ref, count_ref, perm_ref, cotangent, raw, merged, table, index, near, acc, part, part_in, gt, twin, twin_in, summed,
    y_in, z_out, z_in, z_far, z_half, far_in, half_in, relay, relay_in, q_out, q_in,
    w1, w1_in, w2, w2_in, w3, w4, local_sem, send_sem, recv_sem,
):
    row, x = lax.axis_index("row"), lax.axis_index("col")
    z, y, core = row // (2 * NY), (row // 2) % NY, row % 2

    def device(dz, dy, dc=0, dx=0):
        there = ((z + dz + NZ) % NZ * NY + (y + dy + NY) % NY) * 2 + (core + dc) % 2
        return there, (x + dx) % NX

    mine8 = y * 2 + core

    def octet(step):
        there = (mine8 + step) % 8
        return (z * NY + there // 2) * 2 + there % 2, x

    lists = [(rows_in, rows_ref), (cols_in, cols_ref), (count_in, count_ref), (perm_in, perm_ref)]
    lists = [pltpu.make_async_copy(*pair, local_sem.at[9 + k]) for k, pair in enumerate(lists)]
    for copy in lists:
        copy.start()
    barrier = pltpu.get_barrier_semaphore()
    peers = [device(dz, 0) for dz in range(1, NZ)] + [octet(step) for step in range(1, 8)]
    peers += [device(0, 0, 0, dx) for dx in range(1, NX)]
    for peer in peers:
        pl.semaphore_signal(barrier, inc=1, device_id=peer, device_id_type=MESH)
    fetches = [pltpu.make_async_copy(features, near.at[0, 0, 0], local_sem.at[13])]
    for part_no in range(8):
        some = pl.ds(part_no * (TCAP // 8), TCAP // 8)
        fetches.append(pltpu.make_async_copy(tiles.at[0, 0, some], raw.at[some], local_sem.at[part_no]))
    fetches.append(pltpu.make_async_copy(weight_in, weight, local_sem.at[14]))
    fetches.append(pltpu.make_async_copy(cotangent_in, cotangent, local_sem.at[15]))
    for fetch in fetches:
        fetch.start()
    for copy in lists:
        copy.wait()
    prepare(rows_ref, cols_ref, count_ref, perm_ref, table)
    to_scalar = pltpu.make_async_copy(table, index, local_sem.at[8])
    to_scalar.start()
    acc[...] = jnp.zeros_like(acc)
    pl.semaphore_wait(barrier, len(peers))

    sends = Sends(send_sem, recv_sem, device(0, 0, 1))
    sibling = device(0, 0, 1)

    def block(oz, oy, piece):
        return near.at[oz % NZ, oy % NY, 0, pl.ds(piece[0], piece[1]), :]

    g1, g1a, g1b = (0, G1), (0, G1A), (G1A, G1 - G1A)
    g2, g2a, g2b = (G1, G2), (G1, G2A), (G1 + G2A, G2 - G2A)

    def pass_on(name, oz, oy, piece, dz, dy):
        source = features.at[pl.ds(piece[0], piece[1]), :] if (oz, oy) == (0, 0) else block(oz, oy, piece)
        sends.start(name, source, block(oz - dz, oy - dy, piece), device(dz, dy))

    def along_y(oz, relayed):
        for dy in (1, -1):
            pass_on(("y", oz, dy), oz, 0, g1, 0, dy)
        if not relayed:
            pass_on(("y", oz, 2), oz, 0, g1, 0, 2)

    def along_y_more(oz):
        for s, half in ((1, g1a), (-1, g1b)):
            sends.wait(("y", oz, s))
            pass_on(("y", oz, 2 * s), oz, -s, half, 0, s)

    def along_y_done(oz, relayed):
        for dy in (2, -2) if relayed else (1, -1, 2):
            sends.wait(("y", oz, dy))

    def along_z(name, oy, piece, dzs):
        for dz in dzs:
            pass_on((name, oy, dz), 0, oy, piece, dz, 0)

    def along_z_more(name, oy, piece, halves):
        for s, half in ((1, halves[0]), (-1, halves[1])):
            sends.wait((name, oy, 2 * s))
            pass_on((name, oy, 3 * s), -2 * s, oy, piece, s, 0)
            pass_on((name, oy, 4 * s), -2 * s, oy, half, 2 * s, 0)

    def q_more(oy):
        along_z_more("q", oy, g2, (g2a, g2b))

    def q_done(*dzs):
        for oy in (0, -1, 1, 2):
            for dz in dzs:
                sends.wait(("q", oy, dz))

    def share(oz):
        sends.start(("s", oz), near.at[oz % NZ, :, 0], near.at[oz % NZ, :, 1], sibling)

    def shared(*ozs):
        for oz in ozs:
            sends.wait(("s", oz))

    def column(dzi, dyi, other):
        there = (((z + dzi) % NZ) * NY + (y + dyi) % NY) * 2 + (core + other) % 2
        return there * 2

    def forward(first, second, other):
        def step(number, carry):
            dzi = first + (second - first) * number
            for part_no in range(0, ROWBLK, 4):
                sum_ = jnp.zeros((4 * BS, F), F32)
                for dyi in range(NY):
                    where = column(dzi, dyi, other)
                    left = [merged[pick(index, 0, rb * 128 + where, TCAP)] for rb in range(part_no, part_no + 4)]
                    right = [merged[pick(index, 0, rb * 128 + where + 1, TCAP)] for rb in range(part_no, part_no + 4)]
                    both = jnp.concatenate([jnp.concatenate(left, axis=0), jnp.concatenate(right, axis=0)], axis=1)
                    sum_ += jnp.dot(both, near[dzi, dyi, other], preferred_element_type=F32)
                acc[pl.ds(part_no, 4)] += sum_.reshape(4, BS, F)
            return carry

        lax.fori_loop(0, 1 if first == second else 2, step, 0)

    along_z("z", 0, g1, (2, -2, 1, -1))
    for s in (1, -1):
        pass_on(("p", s), 0, 0, g2, 0, s)
    along_y(0, True)
    pass_on(("p", 2), 0, 0, g2, 0, 2)
    along_z("q", 0, g2, (2, -2, 1, -1))
    to_scalar.wait()
    for fetch in fetches:
        fetch.wait()
    merge(index, raw, merged)
    for s in (1, -1):
        sends.wait(("z", 0, s))
        along_y(-s, True)
    along_z_more("z", 0, g1, (g1a, g1b))
    for s in (1, -1):
        sends.wait(("p", s))
        along_z("q", -s, g2, (2, -2, 1, -1))
    sends.wait(("p", 2))
    along_z("q", 2, g2, (2, -2, 1, -1))
    for s in (1, -1):
        along_y(2 * s, True)
    along_y_more(0)
    q_more(0)
    along_y_more(-1)
    along_y_more(1)
    for s in (1, -1):
        sends.wait(("z", 0, 3 * s))
        along_y(-3 * s, False)
    for s in (1, -1):
        sends.wait(("z", 0, 4 * s))
    along_y(4, False)
    q_more(-1)
    q_more(1)
    along_y_done(0, True)
    share(0)
    along_y_more(-2)
    along_y_more(2)
    q_more(2)
    forward(0, 0, 0)
    q_done(1, -1)
    for oz in (-1, 1):
        along_y_done(oz, True)
        share(oz)
    shared(0)
    forward(0, 0, 1)
    forward(1, 7, 0)
    for oz in (-2, 2):
        along_y_done(oz, True)
        share(oz)
    shared(1, -1)
    forward(1, 7, 1)
    forward(2, 6, 0)
    shared(2, -2)
    forward(2, 6, 1)
    q_done(3, -3)
    for oz in (-3, 3):
        along_y_done(oz, False)
        share(oz)
    forward(3, 5, 0)
    q_done(4, -4)
    along_y_done(4, False)
    share(4)
    shared(3, -3)
    forward(3, 5, 1)
    forward(4, 4, 0)
    shared(4)
    forward(4, 4, 1)

    for dx in (2, 1, 3):
        there = (x + dx) % NX
        part[dx] = acc[pl.ds(there * 2, 2)].reshape(ROWS, F).astype(BF)
        sends.start(("part", dx), part.at[dx], part_in.at[dx], device(0, 0, 0, dx))
    total = acc[pl.ds(x * 2, 2)].reshape(ROWS, F)
    for dx in (1, 3, 2):
        sends.wait(("part", dx))
        total += part_in[dx].astype(F32)
    aggregated = total.astype(BF)
    pre = jnp.dot(aggregated, weight[...], preferred_element_type=F32)
    square = pre * pre
    bend = jnp.tanh(GELU * (pre + 0.044715 * (square * pre)))
    slope = 0.5 * (1.0 + bend) + (0.5 * GELU) * pre * (1.0 - bend * bend) * (1.0 + 3.0 * 0.044715 * square)
    grad_pre = (cotangent[...].astype(F32) * slope).astype(BF)
    gt[0] = lax.dot_general(weight[...], grad_pre, (((1,), (1,)), ((), ())), preferred_element_type=F32).astype(BF)
    for dx in (2, 1, 3):
        sends.start(("gt", dx), gt.at[0], gt.at[NX - dx], device(0, 0, 0, dx))
    activation[...] = (0.5 * pre * (1.0 + bend)).astype(BF)
    term = lax.dot_general(aggregated, grad_pre, (((0,), (0,)), ((), ())), preferred_element_type=F32)
    for q in range(NX):
        for j in range(8):
            w1[q, j] = term[q * 32 + j % 4 * 8:q * 32 + j % 4 * 8 + 8, j // 4 * 128:j // 4 * 128 + 128]
    for dx in (2, 1, 3):
        sends.start(("w1", dx), w1.at[(x + dx) % NX], w1_in.at[dx], device(0, 0, 0, dx))
    for dx in (1, 3, 2):
        sends.wait(("gt", dx))

    def backward(first, second, other):
        def step(number, carry):
            dzi = first + (second - first) * number
            for dyi in range(NY):
                where = column(dzi, dyi, other)
                sum_ = jnp.zeros((F, ROWS), F32)
                for dx in range(NX):
                    base = (x + dx) % NX * 2 * 128 + where
                    corners = [merged[pick(index, 0, base + a, TCAP)] for a in (0, 1, 128, 129)]
                    grid = jnp.concatenate([jnp.concatenate(corners[:2], axis=1), jnp.concatenate(corners[2:], axis=1)], axis=0)
                    sum_ += jnp.dot(gt[dx], grid, preferred_element_type=F32)
                if other:
                    twin[dzi, dyi] = sum_.astype(BF)
                else:
                    summed[dzi, dyi] = (sum_ + twin_in[dzi, dyi].astype(F32)).astype(BF)
            return carry

        lax.fori_loop(0, 1 if first == second else 2, step, 0)

    r1, r1a, r1b = pl.ds(0, R1), pl.ds(0, R1A), pl.ds(R1A, R1 - R1A)
    r2, r2a, r2b = pl.ds(R1, R2), pl.ds(R1, R2A), pl.ds(R1 + R2A, R2 - R2A)
    dys = (1, 3, 2)

    def for_twin(*group):
        backward(group[0], group[-1], 1)
        for dzi in group:
            sends.start(("t", dzi), twin.at[dzi], twin_in.at[dzi], sibling)

    def for_plane(*group):
        for dzi in group:
            sends.wait(("t", dzi))
        backward(group[0], group[-1], 0)
        for dzi in group:
            for k, dy in enumerate(dys):
                sends.start(("Y", dzi, k), summed.at[dzi, dy, r1], y_in.at[dzi, k], device(0, dy))
        for dzi in group:
            for dy in range(NY):
                if dzi == 4:
                    sends.start(("half", 0, dy), summed.at[4, dy, r2a], half_in.at[0, dy, pl.ds(0, R2A)], device(2, 0))
                    sends.start(("half", 1, dy), summed.at[4, dy, r2b], half_in.at[1, dy, pl.ds(0, R2 - R2A)], device(-2, 0))
                elif dzi in (3, 5):
                    s = 0 if dzi == 3 else 1
                    sends.start(("far", s, dy), summed.at[dzi, dy, r2], far_in.at[s, dy], device(1 - 2 * s, 0))
                elif dzi in (1, 7):
                    s = 0 if dzi == 1 else 1
                    sends.start(("q", s, dy), summed.at[dzi, dy, r2], relay_in.at[s, dy], device(1 - 2 * s, 0))

    def relays():
        for s, dzi in ((0, 2), (1, 6)):
            for dy in (1, 3, 2, 0):
                sends.wait(("half", s, dy))
                sends.wait(("far", s, dy))
                relay[s, dy] = (summed[dzi, dy, r2].astype(F32) + far_in[s, dy].astype(F32)).astype(BF)
                some = pl.ds(0, R2A) if s == 0 else pl.ds(R2A, R2 - R2A)
                extra = half_in[s, dy, pl.ds(0, R2A if s == 0 else R2 - R2A)]
                mine = r2a if s == 0 else r2b
                relay[s, dy, some] = (
                    summed[dzi, dy, mine].astype(F32) + far_in[s, dy, some].astype(F32) + extra.astype(F32)
                ).astype(BF)
                sends.start(("q", 2 + s, dy), relay.at[s, dy], relay_in.at[2 + s, dy], device(2 - 4 * s, 0))

    def y_sum(dzi):
        value = summed[dzi, 0, r1].astype(F32)
        for k in range(3):
            sends.wait(("Y", dzi, k))
            value += y_in[dzi, k].astype(F32)
        return value

    def z_stage(dzi):
        value = y_sum(dzi)
        if dzi in (2, 6):
            s = 0 if dzi == 2 else 1
            sends.wait(("Zfar", s))
            sends.wait(("Zhalf", s))
            value += z_far[s].astype(F32)
            some, size = (r1a, R1A) if s == 0 else (r1b, R1 - R1A)
            z_out[dzi] = value.astype(BF)
            extra = z_half[s, pl.ds(0, size)].astype(F32)
            z_out[dzi, some] = (value[some.start:some.start + size] + extra).astype(BF)
        else:
            z_out[dzi] = value.astype(BF)
        if dzi == 4:
            sends.start(("Zhalf", 0), z_out.at[4, r1a], z_half.at[0, pl.ds(0, R1A)], device(2, 0))
            sends.start(("Zhalf", 1), z_out.at[4, r1b], z_half.at[1, pl.ds(0, R1 - R1A)], device(-2, 0))
        elif dzi in (3, 5):
            s = 0 if dzi == 3 else 1
            sends.start(("Zfar", s), z_out.at[dzi], z_far.at[s], device(1 - 2 * s, 0))
        else:
            sends.start(("Z", dzi), z_out.at[dzi], z_in.at[dzi], device(dzi, 0))

    def q_sum(dy):
        value = summed[0, dy, r2].astype(F32)
        for k in range(4):
            sends.wait(("q", k, dy))
            value += relay_in[k, dy].astype(F32)
        return value

    for_twin(4)
    w2[...] = w1[x]
    for dx in (1, 3, 2):
        sends.wait(("w1", dx))
        w2[...] += w1_in[dx]
    for step in range(1, 8):
        sends.start(("w2", step), w2.at[(mine8 + step) % 8], w2_in.at[step], octet(step))
    for_twin(3, 5)
    for_plane(4)
    for_twin(2, 6)
    for_plane(3, 5)
    for_twin(1, 7)
    for_plane(2, 6)
    here = w2[mine8]
    for step in range(1, 8):
        sends.wait(("w2", step))
        here += w2_in[step]
    w3[z] = here
    for dz in range(1, NZ):
        sends.start(("w3", dz), w3.at[z], w3.at[z], device(dz, 0))
    relays()
    z_stage(4)
    for_twin(0)
    for_plane(1, 7)
    for_plane(0)
    z_stage(3)
    z_stage(5)
    for dz in range(1, NZ):
        sends.wait_for(("w3", dz), w3.at[(z + NZ - dz) % NZ])
    here = w3[0]
    for k in range(1, NZ):
        here += w3[k]
    w4[mine8] = here
    for step in range(1, 8):
        sends.start(("w4", step), w4.at[mine8], w4.at[mine8], octet(step))
    z_stage(2)
    z_stage(6)
    for k, dy in enumerate(dys):
        q_out[k] = q_sum(dy).astype(BF)
        sends.start(("Q", k), q_out.at[k], q_in.at[k], device(0, dy))
    for step in range(1, 8):
        sends.wait_for(("w4", step), w4.at[(mine8 + 8 - step) % 8])
    w5[x] = w4[...]
    for dx in (2, 1, 3):
        sends.start(("w5", dx), w4, w5.at[x], device(0, 0, 0, dx))
    z_stage(1)
    z_stage(7)
    top = y_sum(0)
    bottom = q_sum(0)
    for dzi in (2, 6, 1, 7):
        sends.wait(("Z", dzi))
        top += z_in[dzi].astype(F32)
    for k in range(3):
        sends.wait(("Q", k))
        bottom += q_in[k].astype(F32)
    grad_turned[0:R1] = top
    grad_turned[R1:F] = bottom
    for dx in (1, 3, 2):
        sends.wait_for(("w5", dx), w5.at[(x + NX - dx) % NX])
    sends.drain()
    assert not sends.landing


def finish(active, turned, pieces, activation, grad_features, grad_weight):
    activation[...] = active[...]
    grad_features[...] = turned[...].T
    for q in range(NX):
        for j in range(8):
            grad_weight[q * 32 + j % 4 * 8:q * 32 + j % 4 * 8 + 8, j // 4 * 128:j // 4 * 128 + 128] = pieces[q, j]


def body(features, weight, tiles, tile_rows, tile_cols, tile_count, block_perm, cotangent):
    vmem = pl.BlockSpec(memory_space=pltpu.VMEM)
    parts = pl.pallas_call(
        whole,
        out_shape=(
            jax.ShapeDtypeStruct((ROWS, H), BF),
            jax.ShapeDtypeStruct((F, ROWS), F32),
            jax.ShapeDtypeStruct((NX, 8, 8, 128), F32),
        ),
        in_specs=[pl.BlockSpec(memory_space=pltpu.HBM)] * 8,
        out_specs=(vmem, vmem, vmem),
        scratch_shapes=[
            pltpu.VMEM((F, H), BF),
            pltpu.VMEM((1, TCAP), jnp.int32),
            pltpu.VMEM((1, TCAP), jnp.int32),
            pltpu.VMEM((1, 1), jnp.int32),
            pltpu.VMEM((1, NBLK), jnp.int32),
            pltpu.VMEM((ROWS, H), BF),
            pltpu.VMEM((TCAP, BS, BS), BF),
            pltpu.VMEM((TCAP + 1, BS, BS), BF),
            pltpu.VMEM((8, NPLACE), jnp.int32),
            pltpu.SMEM((8, NPLACE), jnp.int32),
            pltpu.VMEM((NZ, NY, 2, ROWS, F), BF),
            pltpu.VMEM((ROWBLK, BS, F), F32),
            pltpu.VMEM((NX, ROWS, F), BF),
            pltpu.VMEM((NX, ROWS, F), BF),
            pltpu.VMEM((NX, F, ROWS), BF),
            pltpu.VMEM((NZ, NY, F, ROWS), BF),
            pltpu.VMEM((NZ, NY, F, ROWS), BF),
            pltpu.VMEM((NZ, NY, F, ROWS), BF),
            pltpu.VMEM((NZ, 3, R1, ROWS), BF),
            pltpu.VMEM((NZ, R1, ROWS), BF),
            pltpu.VMEM((NZ, R1, ROWS), BF),
            pltpu.VMEM((2, R1, ROWS), BF),
            pltpu.VMEM((2, R1 - R1A, ROWS), BF),
            pltpu.VMEM((2, NY, R2, ROWS), BF),
            pltpu.VMEM((2, NY, R2 - R2A, ROWS), BF),
            pltpu.VMEM((2, NY, R2, ROWS), BF),
            pltpu.VMEM((4, NY, R2, ROWS), BF),
            pltpu.VMEM((3, R2, ROWS), BF),
            pltpu.VMEM((3, R2, ROWS), BF),
            pltpu.VMEM((NX, 8, 8, 128), F32),
            pltpu.VMEM((NX, 8, 8, 128), F32),
            pltpu.VMEM((8, 8, 128), F32),
            pltpu.VMEM((8, 8, 128), F32),
            pltpu.VMEM((NZ, 8, 128), F32),
            pltpu.VMEM((8, 8, 128), F32),
            pltpu.SemaphoreType.DMA((16,)),
            pltpu.SemaphoreType.DMA((NSEM,)),
            pltpu.SemaphoreType.DMA((NSEM,)),
        ],
        compiler_params=pltpu.CompilerParams(
            collective_id=0, has_side_effects=True, vmem_limit_bytes=56 * 2**20),
    )(
        features, weight, tiles, tile_rows.reshape(1, TCAP), tile_cols.reshape(1, TCAP), tile_count,
        block_perm.reshape(1, NBLK), cotangent,
    )
    return pl.pallas_call(
        finish,
        out_shape=(
            jax.ShapeDtypeStruct((ROWS, H), BF),
            jax.ShapeDtypeStruct((ROWS, F), F32),
            jax.ShapeDtypeStruct((F, H), F32),
        ),
    )(*parts)


def solution(mesh):
    return jax.shard_map(
        body,
        mesh=mesh,
        in_specs=(
            P(("row", "col"), None),
            P(),
            P("row", "col", None, None, None),
            P("row", "col", None),
            P("row", "col", None),
            P("row", "col"),
            P(),
            P(("row", "col"), None),
        ),
        out_specs=(P(("row", "col"), None), P(("row", "col"), None), P()),
        check_vma=False,
    )
```

time: 109 us -> 82.6 us (0.76)
  Pallas kernels: 103 us -> 81.2 us
  local copies, waits for them, and re-layouts: 4.7 us -> 0 us
    pallas_call x1, Pallas kernels: 103 us -> 79.4 us  [body(): pl.pallas_call(whole, out_shape=(jax.ShapeDtypeStruct((ROWS, H), BF), jax...]
    unnamed x3 -> x0, local copies, waits for them, and re-layouts: 4.7 us -> none
    pallas_call x0 -> x1, Pallas kernels: none -> 1.83 us  [body(): pl.pallas_call(finish, out_shape=(jax.ShapeDtypeStruct((ROWS, H), BF), ja...]
where the time goes in v2:
time: 82.6 us; the launch traced here: 82.5 us
  Pallas kernels  81.2 us (98%)
  between operations  1.29 us (2%)
    pallas_call x1, Pallas kernels, body(): pl.pallas_call(whole, out_shape=(jax.ShapeDtypeStruct((ROWS, H), BF), jax...  79.4 us
    pallas_call x1, Pallas kernels, body(): pl.pallas_call(finish, out_shape=(jax.ShapeDtypeStruct((ROWS, H), BF), ja...  1.83 us

profile of v2, /device:TPU:1, one launch (start us, length us, event | category | flops | bytes accessed | tf_op | source)
XLA Modules:
  0.0 82.5 jit_solution(10585425834600292905)
XLA Ops:
  1.3 79.4 %shard_map.103 = (bf16[256,256]{1,0:T(8,128)(2,1)}, f32[128,256]{1,0:T(8,128)}, f32[4,8,8,128]{3,2,1,0:T(8,128)}) custom-call(bf16[256,128]{1,0:T(8,128)(2,1)} %features.1, bf16[128,256]{1,0:T(8,128)(2,1)} %weight_in.1, bf16[1,1,384,128,128]{4,3,2,1,0:T(8,128)(2,1)} %tiles.1, s32[1,384]{1,0:T(1,128)} %bitcast.4, s32[1,384]{1,0:T(1,128)} %bitcast.5, ...), custom_call_target="tpu_custom_call" | custom-call | tf_op jit(solution)/shard_map/pallas_call | solution.py:483
  80.7 1.8 %shard_map.104 = (bf16[256,256]{1,0:T(8,128)(2,1)}, f32[256,128]{1,0:T(8,128)}, f32[128,256]{1,0:T(8,128)}) custom-call(bf16[256,256]{1,0:T(8,128)(2,1)} %get-tuple-element.6.active, f32[128,256]{1,0:T(8,128)} %get-tuple-element.7.turned, f32[4,8,8,128]{3,2,1,0:T(8,128)} %get-tuple-element.8.pieces), custom_call_target="tpu_custom_call" | custom-call | tf_op jit(solution)/shard_map/pallas_call | solution.py:538

commit v3 on v2

--- a/solution.py
+++ b/solution.py
@@ -16,7 +16,7 @@
 TCAP, NBLK, ROWBLK = 384, 512, 8
 NPLACE = 1024
 ROWS = 256
-G1, G1A, G2A, G2 = 176, 80, 48, 80
+G1, G1A, G2A, G2 = 144, 64, 48, 112
 R1, R1A, R2A, R2 = 80, 32, 16, 48
 NSEM = 256
 GELU = math.sqrt(2.0 / math.pi)
@@ -49,6 +49,7 @@
     def drain(self):
         for copy in self.started:
             copy.wait_send()
+        self.started = []
 
 
 def prepare(rows_ref, cols_ref, count_ref, perm_ref, table):
@@ -200,8 +201,7 @@
         return there * 2
 
     def forward(first, second, other):
-        def step(number, carry):
-            dzi = first + (second - first) * number
+        for dzi in (first, second)[:1 if first == second else 2]:
             for part_no in range(0, ROWBLK, 4):
                 sum_ = jnp.zeros((4 * BS, F), F32)
                 for dyi in range(NY):
@@ -211,9 +211,6 @@
                     both = jnp.concatenate([jnp.concatenate(left, axis=0), jnp.concatenate(right, axis=0)], axis=1)
                     sum_ += jnp.dot(both, near[dzi, dyi, other], preferred_element_type=F32)
                 acc[pl.ds(part_no, 4)] += sum_.reshape(4, BS, F)
-            return carry
-
-        lax.fori_loop(0, 1 if first == second else 2, step, 0)
 
     along_z("z", 0, g1, (2, -2, 1, -1))
     for s in (1, -1):
@@ -307,6 +304,7 @@
             w1[q, j] = term[q * 32 + j % 4 * 8:q * 32 + j % 4 * 8 + 8, j // 4 * 128:j // 4 * 128 + 128]
     for dx in (2, 1, 3):
         sends.start(("w1", dx), w1.at[(x + dx) % NX], w1_in.at[dx], device(0, 0, 0, dx))
+    sends.drain()
     for dx in (1, 3, 2):
         sends.wait(("gt", dx))
 
@@ -346,30 +344,27 @@
             for k, dy in enumerate(dys):
                 sends.start(("Y", dzi, k), summed.at[dzi, dy, r1], y_in.at[dzi, k], device(0, dy))
         for dzi in group:
-            for dy in range(NY):
-                if dzi == 4:
-                    sends.start(("half", 0, dy), summed.at[4, dy, r2a], half_in.at[0, dy, pl.ds(0, R2A)], device(2, 0))
-                    sends.start(("half", 1, dy), summed.at[4, dy, r2b], half_in.at[1, dy, pl.ds(0, R2 - R2A)], device(-2, 0))
-                elif dzi in (3, 5):
-                    s = 0 if dzi == 3 else 1
-                    sends.start(("far", s, dy), summed.at[dzi, dy, r2], far_in.at[s, dy], device(1 - 2 * s, 0))
-                elif dzi in (1, 7):
-                    s = 0 if dzi == 1 else 1
-                    sends.start(("q", s, dy), summed.at[dzi, dy, r2], relay_in.at[s, dy], device(1 - 2 * s, 0))
+            if dzi == 4:
+                sends.start(("half", 0), summed.at[4, :, r2a], half_in.at[0, :, pl.ds(0, R2A)], device(2, 0))
+                sends.start(("half", 1), summed.at[4, :, r2b], half_in.at[1, :, pl.ds(0, R2 - R2A)], device(-2, 0))
+            elif dzi in (3, 5):
+                s = 0 if dzi == 3 else 1
+                sends.start(("far", s), summed.at[dzi, :, r2], far_in.at[s], device(1 - 2 * s, 0))
+            elif dzi in (1, 7):
+                s = 0 if dzi == 1 else 1
+                sends.start(("q", s), summed.at[dzi, :, r2], relay_in.at[s], device(1 - 2 * s, 0))
 
     def relays():
         for s, dzi in ((0, 2), (1, 6)):
-            for dy in (1, 3, 2, 0):
-                sends.wait(("half", s, dy))
-                sends.wait(("far", s, dy))
-                relay[s, dy] = (summed[dzi, dy, r2].astype(F32) + far_in[s, dy].astype(F32)).astype(BF)
-                some = pl.ds(0, R2A) if s == 0 else pl.ds(R2A, R2 - R2A)
-                extra = half_in[s, dy, pl.ds(0, R2A if s == 0 else R2 - R2A)]
-                mine = r2a if s == 0 else r2b
-                relay[s, dy, some] = (
-                    summed[dzi, dy, mine].astype(F32) + far_in[s, dy, some].astype(F32) + extra.astype(F32)
-                ).astype(BF)
-                sends.start(("q", 2 + s, dy), relay.at[s, dy], relay_in.at[2 + s, dy], device(2 - 4 * s, 0))
+            sends.wait(("half", s))
+            sends.wait(("far", s))
+            size = R2A if s == 0 else R2 - R2A
+            start = 0 if s == 0 else R2A
+            value = summed[dzi, :, r2].astype(F32) + far_in[s].astype(F32)
+            relay[s] = value.astype(BF)
+            extra = half_in[s, :, pl.ds(0, size)].astype(F32)
+            relay[s, :, pl.ds(start, size)] = (value[:, start:start + size] + extra).astype(BF)
+            sends.start(("q", 2 + s), relay.at[s], relay_in.at[2 + s], device(2 - 4 * s, 0))
 
     def y_sum(dzi):
         value = summed[dzi, 0, r1].astype(F32)
@@ -403,7 +398,6 @@
     def q_sum(dy):
         value = summed[0, dy, r2].astype(F32)
         for k in range(4):
-            sends.wait(("q", k, dy))
             value += relay_in[k, dy].astype(F32)
         return value
 
@@ -444,6 +438,8 @@
         sends.start(("w4", step), w4.at[mine8], w4.at[mine8], octet(step))
     z_stage(2)
     z_stage(6)
+    for k in range(4):
+        sends.wait(("q", k))
     for k, dy in enumerate(dys):
         q_out[k] = q_sum(dy).astype(BF)
         sends.start(("Q", k), q_out.at[k], q_in.at[k], device(0, dy))
@@ -456,6 +452,7 @@
     z_stage(7)
     top = y_sum(0)
     bottom = q_sum(0)
+    sends.drain()
     for dzi in (2, 6, 1, 7):
         sends.wait(("Z", dzi))
         top += z_in[dzi].astype(F32)

time: 82.6 us -> 79.3 us (0.960)
  Pallas kernels: 81.2 us -> 77.9 us
    pallas_call x1, Pallas kernels: 79.4 us -> 76.1 us  [body(): pl.pallas_call(whole, out_shape=(jax.ShapeDtypeStruct((ROWS, H), BF), jax...]
where the time goes in v3:
time: 79.3 us; the launch traced here: 79.2 us
  Pallas kernels  77.9 us (98%)
  between operations  1.29 us (2%)
    pallas_call x1, Pallas kernels, body(): pl.pallas_call(whole, out_shape=(jax.ShapeDtypeStruct((ROWS, H), BF), jax...  76.1 us
    pallas_call x1, Pallas kernels, body(): pl.pallas_call(finish, out_shape=(jax.ShapeDtypeStruct((ROWS, H), BF), ja...  1.83 us

profile of v3, /device:TPU:1, one launch (start us, length us, event | category | flops | bytes accessed | tf_op | source)
XLA Modules:
  0.0 79.2 jit_solution(8642533745661951289)
XLA Ops:
  1.3 76.1 %shard_map.103 = (bf16[256,256]{1,0:T(8,128)(2,1)}, f32[128,256]{1,0:T(8,128)}, f32[4,8,8,128]{3,2,1,0:T(8,128)}) custom-call(bf16[256,128]{1,0:T(8,128)(2,1)} %features.1, bf16[128,256]{1,0:T(8,128)(2,1)} %weight_in.1, bf16[1,1,384,128,128]{4,3,2,1,0:T(8,128)(2,1)} %tiles.1, s32[1,384]{1,0:T(1,128)} %bitcast.4, s32[1,384]{1,0:T(1,128)} %bitcast.5, ...), custom_call_target="tpu_custom_call" | custom-call | tf_op jit(solution)/shard_map/pallas_call | solution.py:480
  77.4 1.8 %shard_map.104 = (bf16[256,256]{1,0:T(8,128)(2,1)}, f32[256,128]{1,0:T(8,128)}, f32[128,256]{1,0:T(8,128)}) custom-call(bf16[256,256]{1,0:T(8,128)(2,1)} %get-tuple-element.6.active, f32[128,256]{1,0:T(8,128)} %get-tuple-element.7.turned, f32[4,8,8,128]{3,2,1,0:T(8,128)} %get-tuple-element.8.pieces), custom_call_target="tpu_custom_call" | custom-call | tf_op jit(solution)/shard_map/pallas_call | solution.py:535
